TPU v7x, 256 devices: a whole 4x4x8 slice. The times are simulated.
256 devices in a mesh: row: 8 (over z_lo, core), col: 32 (over y, x, z_hi).
Axes of the slice: x: 4, y: 4, z: 8 (z_hi: 2, z_lo: 4; z = z_hi * 4 + z_lo), core: 2. Of those that a mesh axis runs over, the one named last changes fastest.
Arguments:
- pair: bfloat16 [32, 8, 2, 512, 128], P(None, 'row', None, 'col'), may hold values from -5 to 5
- w_query: bfloat16 [2, 2, 128, 256], replicated, may hold values from -4 to 4
- w_key: bfloat16 [2, 2, 128, 256], replicated, may hold values from -4 to 4
- w_value: bfloat16 [2, 2, 128, 256], replicated, may hold values from -0.5 to 0.5
- w_gate: bfloat16 [2, 2, 128, 256], replicated, may hold values from -0.5 to 0.5
- w_out: bfloat16 [2, 2, 256, 128], replicated, may hold values from -3 to 3
- w_in: bfloat16 [2, 128, 512], replicated, may hold values from -0.5 to 0.5
- w_back: bfloat16 [2, 512, 128], replicated, may hold values from -0.25 to 0.25
Outputs:
- pair_out: bfloat16 [32, 8, 2, 512, 128], P(None, 'row', None, 'col')
All inputs are finite; a program needn't handle non-finite values.
Results may differ from a plain program's by a relative error of at most 0.03.
Values may be sent and summed in bfloat16 or wider, within the bound.
A program may use at most 64 MiB of HBM per device.

v0:
```python
import jax
import jax.numpy as jnp
from jax import lax
from jax.sharding import PartitionSpec as P

HEADS = 8
HEAD_DIM = 32


epsilon = 1e-05


def layer_norm(values):
    wide = values.astype(jnp.float32)
    center = wide - jnp.mean(wide, axis=-1, keepdims=True)
    spread = jnp.mean(center * center, axis=-1, keepdims=True)
    return (center * lax.rsqrt(spread + epsilon)).astype(jnp.bfloat16)


def split_heads(matrix):
    return matrix.reshape(matrix.shape[0], HEADS, matrix.shape[1] // HEADS)


def attend(normed, weights, direction, pattern):
    project = pattern + ",chd->ehqd"
    queries = jnp.einsum(
        project, normed, split_heads(weights[0][direction]), preferred_element_type=jnp.float32
    ).astype(jnp.bfloat16)
    key_rows = jnp.einsum(
        project, normed, split_heads(weights[1][direction]), preferred_element_type=jnp.float32
    ).astype(jnp.bfloat16)
    value_rows = jnp.einsum(
        project, normed, split_heads(weights[2][direction]), preferred_element_type=jnp.float32
    ).astype(jnp.bfloat16)
    gating = jax.nn.sigmoid(
        jnp.einsum(
            project, normed, split_heads(weights[3][direction]), preferred_element_type=jnp.float32
        )
    )
    scores = jnp.einsum(
        "ehqd,ehkd->ehqk", queries, key_rows, preferred_element_type=jnp.float32
    ) * HEAD_DIM ** (-0.5)
    maximum = jnp.max(scores, axis=-1, keepdims=True)
    exponent = jnp.exp(scores - maximum)
    denominator = jnp.sum(exponent, axis=-1, keepdims=True)
    blended = (
        jnp.einsum(
            "ehqk,ehkd->ehqd",
            exponent.astype(jnp.bfloat16),
            value_rows,
            preferred_element_type=jnp.float32,
        )
        / denominator
    )
    gated_out = (gating * blended).astype(jnp.bfloat16)
    out_matrix = weights[4][direction]
    out_heads = out_matrix.reshape(HEADS, out_matrix.shape[0] // HEADS, out_matrix.shape[1])
    return jnp.einsum(
        "ehqd,hdc->" + pattern, gated_out, out_heads, preferred_element_type=jnp.float32
    )


def local(pair, w_query, w_key, w_value, w_gate, w_out, w_in, w_back):
    row_count = lax.axis_size("row")
    col_count = lax.axis_size("col")
    span_rows = pair.shape[2]
    col_width = pair.shape[3]
    channels = pair.shape[4]
    length = col_count * col_width
    pair_tile = pair.reshape(col_count, span_rows, col_width, channels)

    def layer_step(pair_tile, layer_weights):
        attn_weights = layer_weights[:5]
        row_slab = lax.all_to_all(
            pair_tile, "col", split_axis=0, concat_axis=2, tiled=True
        ).reshape(span_rows, length, channels)
        row_update = attend(layer_norm(row_slab), attn_weights, 0, "eqc")
        row_slab = (row_slab.astype(jnp.float32) + row_update).astype(jnp.bfloat16)
        pair_tile = lax.all_to_all(
            row_slab.reshape(1, span_rows, length, channels),
            "col",
            split_axis=2,
            concat_axis=0,
            tiled=True,
        )
        pair_tile = pair_tile.reshape(col_count, span_rows, row_count, span_rows, channels)
        col_slab = lax.all_to_all(pair_tile, "row", split_axis=2, concat_axis=1, tiled=True)
        col_slab = col_slab.reshape(length, span_rows, channels)
        col_update = attend(layer_norm(col_slab), attn_weights, 1, "qec")
        col_slab = (col_slab.astype(jnp.float32) + col_update).astype(jnp.bfloat16)
        pair_tile = lax.all_to_all(
            col_slab.reshape(col_count, row_count * span_rows, 1, span_rows, channels),
            "row",
            split_axis=1,
            concat_axis=2,
            tiled=True,
        )
        pair_tile = pair_tile.reshape(col_count, span_rows, col_width, channels)
        column_view = lax.all_to_all(
            pair_tile.reshape(col_count, span_rows, row_count, span_rows, channels),
            "row",
            split_axis=2,
            concat_axis=1,
            tiled=True,
        )
        column_view = column_view.reshape(length, span_rows, channels)
        mirrored = lax.all_to_all(
            column_view.reshape(col_count, col_width, span_rows, channels),
            "col",
            split_axis=0,
            concat_axis=2,
            tiled=True,
        )
        mirrored = jnp.transpose(
            mirrored.reshape(col_width, col_count * span_rows, channels), (1, 0, 2)
        )
        mirrored = mirrored.reshape(col_count, span_rows, col_width, channels)
        symmetric = (0.5 * (pair_tile.astype(jnp.float32) + mirrored.astype(jnp.float32))).astype(
            jnp.bfloat16
        )
        normed = layer_norm(symmetric)
        hidden = jax.nn.relu(
            jnp.einsum(
                "aewc,cf->aewf", normed, layer_weights[5], preferred_element_type=jnp.float32
            )
        ).astype(jnp.bfloat16)
        ff_out = jnp.einsum(
            "aewf,fc->aewc", hidden, layer_weights[6], preferred_element_type=jnp.float32
        )
        pair_tile = (symmetric.astype(jnp.float32) + ff_out).astype(jnp.bfloat16)
        return (pair_tile, None)

    final_tile, unused = lax.scan(
        layer_step, pair_tile, (w_query, w_key, w_value, w_gate, w_out, w_in, w_back)
    )
    return final_tile.reshape(pair.shape)


def solution(mesh):
    return jax.shard_map(
        local,
        mesh=mesh,
        in_specs=(P(None, "row", None, "col", None), P(), P(), P(), P(), P(), P(), P()),
        out_specs=P(None, "row", None, "col", None),
        check_vma=False,
    )
```

profile of v0, /device:TPU:1, one launch (start us, length us, event | category | flops | bytes accessed | tf_op | source)
XLA Modules:
  0.0 308.1 jit_solution(1938653983252983169)
XLA Ops:
  1.7 306.5 %while.10 = (s32[]{:T(128)}, bf16[32,2,16,128]{3,2,1,0:T(8,128)(2,1)}, bf16[2,2,128,256]{3,2,1,0:T(8,128)(2,1)}, bf16[2,2,128,256]{3,2,1,0:T(8,128)(2,1)}, bf16[...) while((s32[]{:T(128)}, ...), condition=%wide.region_11.12_spmd, body=%wide.region_0.11_spmd.sunk | while | flops 2092403712 | bytes 137147728 | solution.py:133
  1.7 14.5 %all-to-all-start = ((bf16[32,2,16,128]{3,2,1,0:T(8,128)(2,1)}), bf16[32,2,16,128]{3,2,1,0:T(8,128)(2,1)S(1)}, u32[]{:S(2)}, u32[]{:S(2)}) async-start(bf16[32,2,16,128]{3,2,1,0:T(8,128)(2,1)} %get-tuple-element.227), calls=%async_computation | async-start | bytes 524288 | tf_op jit(solution)/shard_map/while/body/eval_jaxpr/all_to_all | solution.py:74
  19.5 9.3 %all-to-all-done = bf16[32,2,16,128]{3,2,1,0:T(8,128)(2,1)S(1)} async-done(((bf16[32,2,16,128]{3,2,1,0:T(8,128)(2,1)}), bf16[32,2,16,128]{3,2,1,0:T(8,128)(2,1)S(1)}, u32[]{:S(2)}, u32[]{:S(2)}) %all-to-all-start) | async-done | bytes 262176 | tf_op jit(solution)/shard_map/while/body/eval_jaxpr/all_to_all | solution.py:74
  30.0 7.3 %multiply_reduce_fusion.9 = (f32[2,8,512]{2,1,0:T(8,128)S(1)}, f32[2,8,512,512]{2,3,1,0:T(8,128)}) fusion(bf16[2,8,512,32]{2,3,1,0:T(8,128)(2,1)S(1)} %fusion.159, bf16[128,8,32,1]{0,2,1,3:T(8,128)(2,1)S(1)} %bitcast.380, bf16[2,512,128,1]{2,1,3,0:T(8,128)(2,1)S(1)} %bitcast.367), kind=kOutput, calls=%fused_computation.3.clone.1 | convolution fusion | flops 344186880 | bytes 17661952 | tf_op jit(solution)/shard_map/while/body/eval_jaxpr/ehqd,ehkd->ehqk/dot_general | solution.py:40
  37.7 8.6 %fusion.162 = f32[2,8,512]{2,1,0:T(8,128)S(1)} fusion(f32[2,8,512,512]{2,3,1,0:T(8,128)} %get-tuple-element.202, f32[2,8,512]{2,1,0:T(8,128)S(1)} %get-tuple-element.203), kind=kLoop, calls=%fused_computation.4.clone.1 | loop fusion | flops 12574720 | bytes 16842752 | tf_op jit(solution)/shard_map/while/body/eval_jaxpr/reduce_sum | solution.py:45
  54.6 15.2 %all_to_all.76 = bf16[1,2,512,128]{3,1,0,2:T(2,128)(2,1)S(1)} all-to-all(bf16[1,2,512,128]{3,1,0,2:T(2,128)(2,1)S(1)} %copy.172), channel_id=1, replica_groups=mesh['row'=8,'col'=32] {'col'}, dimensions={2} | all-to-all | bytes 524288 | tf_op jit(solution)/shard_map/while/body/eval_jaxpr/all_to_all | solution.py:79
  70.7 9.3 %all-to-all-start.2 = ((bf16[32,2,8,2,128]{4,0,3,1,2:T(8,128)(2,1)}), bf16[32,2,8,2,128]{4,0,3,1,2:T(8,128)(2,1)S(1)}, u32[]{:S(2)}, u32[]{:S(2)}) async-start(bf16[32,2,8,2,128]{4,0,3,1,2:T(8,128)(2,1)} %copy.174), calls=%async_computation.2 | async-start | bytes 524288 | tf_op jit(solution)/shard_map/while/body/eval_jaxpr/all_to_all | solution.py:87
  80.5 8.2 %all-to-all-done.2 = bf16[32,2,8,2,128]{4,0,3,1,2:T(8,128)(2,1)S(1)} async-done(((bf16[32,2,8,2,128]{4,0,3,1,2:T(8,128)(2,1)}), bf16[32,2,8,2,128]{4,0,3,1,2:T(8,128)(2,1)S(1)}, u32[]{:S(2)}, u32[]{:S(2)}) %all-to-all-start.2) | async-done | bytes 262176 | tf_op jit(solution)/shard_map/while/body/eval_jaxpr/all_to_all | solution.py:87
  97.6 8.6 %fusion.168 = f32[2,8,512]{2,1,0:T(8,128)S(1)} fusion(f32[2,8,512,512]{2,3,1,0:T(8,128)} %get-tuple-element.209, f32[2,8,512]{2,1,0:T(8,128)S(1)} %get-tuple-element.210), kind=kLoop, calls=%fused_computation.6.clone.1 | loop fusion | flops 12574720 | bytes 16842752 | tf_op jit(solution)/shard_map/while/body/eval_jaxpr/reduce_sum | solution.py:45
  106.5 7.3 %fusion.167 = f32[2,8,512,32]{2,3,1,0:T(8,128)S(1)} fusion(f32[2,8,512,512]{2,3,1,0:T(8,128)} %get-tuple-element.209, f32[2,8,512]{2,1,0:T(8,128)S(1)} %get-tuple-element.210, bf16[2,8,512,32]{2,3,0,1:T(8,128)(2,1)S(1)} %fusion.166), kind=kOutput, calls=%fused_computation.8.clone.1 | convolution fusion | flops 281018368 | bytes 18382848 | tf_op jit(solution)/shard_map/while/body/eval_jaxpr/ehqk,ehkd->ehqd/dot_general | solution.py:47
  115.5 12.2 %all_to_all.77 = bf16[32,16,1,2,128]{4,0,3,2,1:T(8,128)(2,1)S(1)} all-to-all(bf16[32,16,1,2,128]{4,0,3,2,1:T(8,128)(2,1)S(1)} %copy.183), channel_id=1, replica_groups=mesh['row'=8,'col'=32] {'row'}, dimensions={1} | all-to-all | bytes 524288 | tf_op jit(solution)/shard_map/while/body/eval_jaxpr/all_to_all | solution.py:91
  127.6 12.1 %all_to_all.78 = bf16[32,2,8,2,128]{4,0,3,1,2:T(8,128)(2,1)S(1)} all-to-all(bf16[32,2,8,2,128]{4,0,3,1,2:T(8,128)(2,1)S(1)} %bitcast.370), channel_id=1, replica_groups=mesh['row'=8,'col'=32] {'row'}, dimensions={2} | all-to-all | bytes 524288 | tf_op jit(solution)/shard_map/while/body/eval_jaxpr/all_to_all | solution.py:99
  144.8 12.3 %all-to-all-done.5 = bf16[32,16,2,128]{3,2,1,0:T(2,128)(2,1)S(1)} async-done(((bf16[32,16,2,128]{3,2,1,0:T(2,128)(2,1)}), bf16[32,16,2,128]{3,2,1,0:T(2,128)(2,1)S(1)}, u32[]{:S(2)}, u32[]{:S(2)}) %all-to-all-start.5) | async-done | bytes 262176 | tf_op jit(solution)/shard_map/while/body/eval_jaxpr/all_to_all | solution.py:107
  167.1 8.9 %all-to-all-done = bf16[32,2,16,128]{3,2,1,0:T(8,128)(2,1)S(1)} async-done(((bf16[32,2,16,128]{3,2,1,0:T(8,128)(2,1)}), bf16[32,2,16,128]{3,2,1,0:T(8,128)(2,1)S(1)}, u32[]{:S(2)}, u32[]{:S(2)}) %all-to-all-start) | async-done | bytes 262176 | tf_op jit(solution)/shard_map/while/body/eval_jaxpr/all_to_all | solution.py:74
  184.8 8.6 %fusion.162 = f32[2,8,512]{2,1,0:T(8,128)S(1)} fusion(f32[2,8,512,512]{2,3,1,0:T(8,128)} %get-tuple-element.202, f32[2,8,512]{2,1,0:T(8,128)S(1)} %get-tuple-element.203), kind=kLoop, calls=%fused_computation.4.clone.1 | loop fusion | flops 12574720 | bytes 16842752 | tf_op jit(solution)/shard_map/while/body/eval_jaxpr/reduce_sum | solution.py:45
  201.8 15.5 %all_to_all.76 = bf16[1,2,512,128]{3,1,0,2:T(2,128)(2,1)S(1)} all-to-all(bf16[1,2,512,128]{3,1,0,2:T(2,128)(2,1)S(1)} %copy.172), channel_id=1, replica_groups=mesh['row'=8,'col'=32] {'col'}, dimensions={2} | all-to-all | bytes 524288 | tf_op jit(solution)/shard_map/while/body/eval_jaxpr/all_to_all | solution.py:79
  218.2 10.1 %all-to-all-start.2 = ((bf16[32,2,8,2,128]{4,0,3,1,2:T(8,128)(2,1)}), bf16[32,2,8,2,128]{4,0,3,1,2:T(8,128)(2,1)S(1)}, u32[]{:S(2)}, u32[]{:S(2)}) async-start(bf16[32,2,8,2,128]{4,0,3,1,2:T(8,128)(2,1)} %copy.174), calls=%async_computation.2 | async-start | bytes 524288 | tf_op jit(solution)/shard_map/while/body/eval_jaxpr/all_to_all | solution.py:87
  228.7 8.2 %all-to-all-done.2 = bf16[32,2,8,2,128]{4,0,3,1,2:T(8,128)(2,1)S(1)} async-done(((bf16[32,2,8,2,128]{4,0,3,1,2:T(8,128)(2,1)}), bf16[32,2,8,2,128]{4,0,3,1,2:T(8,128)(2,1)S(1)}, u32[]{:S(2)}, u32[]{:S(2)}) %all-to-all-start.2) | async-done | bytes 262176 | tf_op jit(solution)/shard_map/while/body/eval_jaxpr/all_to_all | solution.py:87
  238.5 7.3 %multiply_reduce_fusion.11 = (f32[2,8,512]{2,1,0:T(8,128)S(1)}, f32[2,8,512,512]{2,3,1,0:T(8,128)}) fusion(bf16[2,8,512,32]{2,3,1,0:T(8,128)(2,1)S(1)} %fusion.165, bf16[128,8,32,1]{0,2,1,3:T(8,128)(2,1)S(1)} %bitcast.381, bf16[512,2,128,1]{2,0,3,1:T(8,128)(2,1)S(1)} %bitcast.363), kind=kOutput, calls=%fused_computation.2.clone.1 | convolution fusion | flops 344186880 | bytes 17661952 | tf_op jit(solution)/shard_map/while/body/eval_jaxpr/ehqd,ehkd->ehqk/dot_general | solution.py:40
  245.9 8.6 %fusion.168 = f32[2,8,512]{2,1,0:T(8,128)S(1)} fusion(f32[2,8,512,512]{2,3,1,0:T(8,128)} %get-tuple-element.209, f32[2,8,512]{2,1,0:T(8,128)S(1)} %get-tuple-element.210), kind=kLoop, calls=%fused_computation.6.clone.1 | loop fusion | flops 12574720 | bytes 16842752 | tf_op jit(solution)/shard_map/while/body/eval_jaxpr/reduce_sum | solution.py:45
  254.8 7.3 %fusion.167 = f32[2,8,512,32]{2,3,1,0:T(8,128)S(1)} fusion(f32[2,8,512,512]{2,3,1,0:T(8,128)} %get-tuple-element.209, f32[2,8,512]{2,1,0:T(8,128)S(1)} %get-tuple-element.210, bf16[2,8,512,32]{2,3,0,1:T(8,128)(2,1)S(1)} %fusion.166), kind=kOutput, calls=%fused_computation.8.clone.1 | convolution fusion | flops 281018368 | bytes 18382848 | tf_op jit(solution)/shard_map/while/body/eval_jaxpr/ehqk,ehkd->ehqd/dot_general | solution.py:47
  263.7 12.2 %all_to_all.77 = bf16[32,16,1,2,128]{4,0,3,2,1:T(8,128)(2,1)S(1)} all-to-all(bf16[32,16,1,2,128]{4,0,3,2,1:T(8,128)(2,1)S(1)} %copy.183), channel_id=1, replica_groups=mesh['row'=8,'col'=32] {'row'}, dimensions={1} | all-to-all | bytes 524288 | tf_op jit(solution)/shard_map/while/body/eval_jaxpr/all_to_all | solution.py:91
  275.9 12.1 %all_to_all.78 = bf16[32,2,8,2,128]{4,0,3,1,2:T(8,128)(2,1)S(1)} all-to-all(bf16[32,2,8,2,128]{4,0,3,1,2:T(8,128)(2,1)S(1)} %bitcast.370), channel_id=1, replica_groups=mesh['row'=8,'col'=32] {'row'}, dimensions={2} | all-to-all | bytes 524288 | tf_op jit(solution)/shard_map/while/body/eval_jaxpr/all_to_all | solution.py:99
  293.1 12.3 %all-to-all-done.5 = bf16[32,16,2,128]{3,2,1,0:T(2,128)(2,1)S(1)} async-done(((bf16[32,16,2,128]{3,2,1,0:T(2,128)(2,1)}), bf16[32,16,2,128]{3,2,1,0:T(2,128)(2,1)S(1)}, u32[]{:S(2)}, u32[]{:S(2)}) %all-to-all-start.5) | async-done | bytes 262176 | tf_op jit(solution)/shard_map/while/body/eval_jaxpr/all_to_all | solution.py:107
  (110 shorter events, 71.5 us)
Async XLA Ops:
  1.7 27.1 %all-to-all-start = ((bf16[32,2,16,128]{3,2,1,0:T(8,128)(2,1)}), bf16[32,2,16,128]{3,2,1,0:T(8,128)(2,1)S(1)}, u32[]{:S(2)}, u32[]{:S(2)}) async-start(bf16[32,2,16,128]{3,2,1,0:T(8,128)(2,1)} %get-tuple-element.227), calls=%async_computation | async-start | bytes 524288 | tf_op jit(solution)/shard_map/while/body/eval_jaxpr/all_to_all | solution.py:74
  70.7 18.0 %all-to-all-start.2 = ((bf16[32,2,8,2,128]{4,0,3,1,2:T(8,128)(2,1)}), bf16[32,2,8,2,128]{4,0,3,1,2:T(8,128)(2,1)S(1)}, u32[]{:S(2)}, u32[]{:S(2)}) async-start(bf16[32,2,8,2,128]{4,0,3,1,2:T(8,128)(2,1)} %copy.174), calls=%async_computation.2 | async-start | bytes 524288 | tf_op jit(solution)/shard_map/while/body/eval_jaxpr/all_to_all | solution.py:87
  106.5 52.0 %copy-start = (bf16[2,128,512]{2,1,0:T(8,128)(2,1)S(1)}, bf16[2,128,512]{2,1,0:T(8,128)(2,1)}, u32[]{:S(2)}) copy-start(bf16[2,128,512]{2,1,0:T(8,128)(2,1)} %get-tuple-element.245) | copy-start | bytes 786436 | tf_op jit(solution)/shard_map/while
  106.5 52.0 %copy-start.1 = (bf16[2,512,128]{2,1,0:T(8,128)(2,1)S(1)}, bf16[2,512,128]{2,1,0:T(8,128)(2,1)}, u32[]{:S(2)}) copy-start(bf16[2,512,128]{2,1,0:T(8,128)(2,1)} %get-tuple-element.246) | copy-start | bytes 786436 | tf_op jit(solution)/shard_map/while
  140.7 16.4 %all-to-all-start.5 = ((bf16[32,16,2,128]{3,2,1,0:T(2,128)(2,1)}), bf16[32,16,2,128]{3,2,1,0:T(2,128)(2,1)S(1)}, u32[]{:S(2)}, u32[]{:S(2)}) async-start(bf16[32,16,2,128]{3,2,1,0:T(2,128)(2,1)} %copy.185), calls=%async_computation.5 | async-start | bytes 524288 | tf_op jit(solution)/shard_map/while/body/eval_jaxpr/all_to_all | solution.py:107
  159.9 16.1 %all-to-all-start = ((bf16[32,2,16,128]{3,2,1,0:T(8,128)(2,1)}), bf16[32,2,16,128]{3,2,1,0:T(8,128)(2,1)S(1)}, u32[]{:S(2)}, u32[]{:S(2)}) async-start(bf16[32,2,16,128]{3,2,1,0:T(8,128)(2,1)} %get-tuple-element.227), calls=%async_computation | async-start | bytes 524288 | tf_op jit(solution)/shard_map/while/body/eval_jaxpr/all_to_all | solution.py:74
  218.2 18.8 %all-to-all-start.2 = ((bf16[32,2,8,2,128]{4,0,3,1,2:T(8,128)(2,1)}), bf16[32,2,8,2,128]{4,0,3,1,2:T(8,128)(2,1)S(1)}, u32[]{:S(2)}, u32[]{:S(2)}) async-start(bf16[32,2,8,2,128]{4,0,3,1,2:T(8,128)(2,1)} %copy.174), calls=%async_computation.2 | async-start | bytes 524288 | tf_op jit(solution)/shard_map/while/body/eval_jaxpr/all_to_all | solution.py:87
  254.7 52.0 %copy-start = (bf16[2,128,512]{2,1,0:T(8,128)(2,1)S(1)}, bf16[2,128,512]{2,1,0:T(8,128)(2,1)}, u32[]{:S(2)}) copy-start(bf16[2,128,512]{2,1,0:T(8,128)(2,1)} %get-tuple-element.245) | copy-start | bytes 786436 | tf_op jit(solution)/shard_map/while
  254.7 52.0 %copy-start.1 = (bf16[2,512,128]{2,1,0:T(8,128)(2,1)S(1)}, bf16[2,512,128]{2,1,0:T(8,128)(2,1)}, u32[]{:S(2)}) copy-start(bf16[2,512,128]{2,1,0:T(8,128)(2,1)} %get-tuple-element.246) | copy-start | bytes 786436 | tf_op jit(solution)/shard_map/while
  288.9 16.4 %all-to-all-start.5 = ((bf16[32,16,2,128]{3,2,1,0:T(2,128)(2,1)}), bf16[32,16,2,128]{3,2,1,0:T(2,128)(2,1)S(1)}, u32[]{:S(2)}, u32[]{:S(2)}) async-start(bf16[32,16,2,128]{3,2,1,0:T(2,128)(2,1)} %copy.185), calls=%async_computation.5 | async-start | bytes 524288 | tf_op jit(solution)/shard_map/while/body/eval_jaxpr/all_to_all | solution.py:107
where the time goes:
time: 311 us; the launch traced here: 308 us
  blocking collectives  79.3 us (25%)
  matrix products  66.6 us (21%)
  waiting for transfers between devices  59.2 us (19%)
  starting transfers between devices  45.5 us (15%)
  other arithmetic  40.8 us (13%)
  local copies, waits for them, and re-layouts  16 us (5%)
    reduce_sum x4, other arithmetic, attend(): denominator = jnp.sum(exponent, axis=-1, keepdims=True)  34.2 us
    all_to_all x2, blocking collectives, layer_step(): lax.all_to_all(row_slab.reshape(1, span_rows, length, channels), 'col', s...  30.8 us
    dot_general x4, matrix products, attend(): jnp.einsum('ehqd,ehkd->ehqk', queries, key_rows, preferred_element_type=j...  29.3 us
    dot_general x4, matrix products, attend(): jnp.einsum('ehqk,ehkd->ehqd', exponent.astype(jnp.bfloat16), value_rows,...  29.2 us
    all_to_all x2, waiting for transfers between devices, layer_step(): lax.all_to_all(column_view.reshape(col_count, col_width, span_rows, chann...  24.6 us
    all_to_all x2, blocking collectives, layer_step(): lax.all_to_all(col_slab.reshape(col_count, row_count * span_rows, 1, span...  24.3 us
    all_to_all x2, blocking collectives, layer_step(): lax.all_to_all(pair_tile.reshape(col_count, span_rows, row_count, span_ro...  24.3 us
    all_to_all x2, starting transfers between devices, layer_step(): lax.all_to_all(pair_tile, 'row', split_axis=2, concat_axis=1, tiled=True)  19.4 us
  transfers between devices with their start and end apart: 6, of which 6 were waited for; matrix products, arithmetic and copies ran while one was open for 3% of the time, Pallas kernels for 0%

commit v1 on v0

v1 whole, which is shorter than its diff:
```python
import math

import jax
import jax.numpy as jnp
from jax import lax
from jax.experimental import pallas as pl
from jax.experimental.pallas import tpu as pltpu
from jax.sharding import PartitionSpec as P

HEADS = 8
HEAD_DIM = 32
INNER = HEADS * HEAD_DIM
CHANNELS = 128
FF = 512
LENGTH = 512
EPSILON = 1e-05
SCALE = math.log2(math.e) / math.sqrt(HEAD_DIM)
MESH = pl.DeviceIdType.MESH
BF = jnp.bfloat16
F32 = jnp.float32
NT = (((1,), (1,)), ((), ()))
TN = (((0,), (0,)), ((), ()))


def layer_norm(wide):
    center = wide - jnp.mean(wide, axis=-1, keepdims=True)
    spread = jnp.mean(center * center, axis=-1, keepdims=True)
    return (center * lax.rsqrt(spread + EPSILON)).astype(BF)


def kernel(
    x, w_query, w_key, w_value, w_gate, w_out, w_in, w_back, out,
    wqt, wvt, wgt, qt, kr, vt, gt, go, grid, mix,
    zr, zc, a_send, a_recv, b_send, b_recv,
    send_sem, in_sem, a_sem, b_sem, t_sem, m_sem,
):
    r = lax.axis_index("row")
    c = lax.axis_index("col")
    core = r % 2
    zl = r // 2
    zv = (zl + 2) % 4
    cy = c // 8
    cx = (c // 2) % 4
    zh = c % 2
    ga = cx * 2 + core
    gb = zv * 8 + cy * 2 + zh
    rd = zv * 2 + core

    def peer_a(g):
        return (zl * 2 + g % 2, cy * 8 + (g // 2) * 2 + zh)

    def peer_b(g):
        return (((g // 8 + 2) % 4) * 2 + core, ((g // 2) % 4) * 8 + cx * 2 + g % 2)

    def copy(src, dst, sem, device):
        return pltpu.make_async_remote_copy(src, dst, send_sem, sem, device_id=device, device_id_type=MESH)

    def loop(start, stop, body):
        lax.fori_loop(start, stop, lambda k, carry: (body(k), carry)[1], 0)

    barrier = pltpu.get_barrier_semaphore()
    loop(0, 32, lambda k: pl.semaphore_signal(barrier, inc=1, device_id=(rd, k), device_id_type=MESH))
    loop(1, 8, lambda k: pl.semaphore_signal(barrier, inc=1, device_id=((r + k) % 8, c), device_id_type=MESH))
    pl.semaphore_wait(barrier, 39)

    place = pl.multiple_of((cx * 8 + cy * 2 + zh) * 16, 16)
    for e in range(2):

        def send_rows(k):
            d = (c + k) % 32
            copy(x.at[d, e], zr.at[e, pl.ds(place, 16)], in_sem.at[e], (rd, d)).start()

        loop(0, 32, send_rows)

    for l in range(2):
        for n in range(2):
            for source, target in ((w_query, wqt), (w_value, wvt), (w_gate, wgt)):
                target[l, n] = source[l, n].astype(F32).T.astype(BF)
    vt[...] = jnp.ones_like(vt)

    def attend(values, l, n):
        wide = values.astype(F32)
        normed = layer_norm(wide)
        qt[...] = (lax.dot_general(wqt[l, n], normed, NT, preferred_element_type=F32) * SCALE).astype(BF)
        kr[...] = jnp.dot(normed, w_key[l, n], preferred_element_type=F32).astype(BF)
        value_rows = lax.dot_general(wvt[l, n], normed, NT, preferred_element_type=F32).astype(BF)
        for h in range(HEADS):
            vt[h, 0:HEAD_DIM, :] = value_rows[h * HEAD_DIM : (h + 1) * HEAD_DIM]
        gt[...] = jax.nn.sigmoid(lax.dot_general(wgt[l, n], normed, NT, preferred_element_type=F32))

        def scores_of(h):
            rows = slice(h * HEAD_DIM, (h + 1) * HEAD_DIM)
            return jnp.dot(kr[:, rows], qt[rows, :], preferred_element_type=F32)

        def probs_of(scores):
            return jnp.exp2(scores - jnp.max(scores, axis=0, keepdims=True)).astype(BF)

        def blend(h, probs):
            rows = slice(h * HEAD_DIM, (h + 1) * HEAD_DIM)
            total = jnp.dot(vt[h], probs, preferred_element_type=F32)
            go[rows, :] = (gt[rows, :] * total[:HEAD_DIM] / total[HEAD_DIM : HEAD_DIM + 1]).astype(BF)

        scores = scores_of(0)
        probs = None
        for h in range(HEADS):
            later = scores_of(h + 1) if h + 1 < HEADS else None
            fresh = probs_of(scores)
            if probs is not None:
                blend(h - 1, probs)
            probs, scores = fresh, later
        blend(HEADS - 1, probs)
        return wide + lax.dot_general(go[...], w_out[l, n], TN, preferred_element_type=F32)

    def transition(wide, l):
        normed = layer_norm(wide)
        hidden = jax.nn.relu(jnp.dot(normed, w_in[l], preferred_element_type=F32)).astype(BF)
        return (wide + jnp.dot(hidden, w_back[l], preferred_element_type=F32)).astype(BF)

    def send_a(ex, e, first_order):
        for g in range(8):
            for t in range(2):
                if first_order:
                    start = (g // 2) * 128 + (g % 2) * 2 + t
                    part = jnp.concatenate(
                        [grid[pl.ds(start + 4 * q, 8, stride=16), :] for q in range(4)], axis=0
                    )
                else:
                    part = grid[pl.ds(g * 2 + t, 32, stride=16), :]
                a_send[ex, g, e, t * 32 : t * 32 + 32, :] = part.astype(BF)

        def go_a(k):
            g = (ga + k) % 8
            copy(a_send.at[ex, g, e], a_recv.at[ex, ga, e], a_sem.at[ex, e], peer_a(g)).start()

        loop(1, 8, go_a)
        a_recv[ex, ga, e] = a_send[ex, ga, e]

    def send_b(ex):
        for e in range(2):
            copy(a_recv.at[ex, pl.ds(0, 7), e], a_recv.at[ex, pl.ds(0, 7), e], a_sem.at[ex, e], (rd, c)).wait_recv()
        for t in range(2):
            for g in range(8):
                for e in range(2):
                    mix[pl.ds(t * 512 + g * 2 + e, 32, stride=16), :] = a_recv[
                        ex, g, e, t * 32 : t * 32 + 32, :
                    ].astype(F32)
            b_send[ex, t] = mix[t * 512 : t * 512 + 512, :].astype(BF)
            mine = pl.multiple_of(gb * 16, 16)

            def go_b(k):
                g = (gb + k) % 32
                rows = pl.ds(pl.multiple_of(g * 16, 16), 16)
                copy(
                    b_send.at[ex, t, rows], b_recv.at[ex, t, pl.ds(mine, 16)], b_sem.at[ex, t], peer_b(g)
                ).start()

            loop(1, 32, go_b)
            b_recv[ex, t, pl.ds(mine, 16)] = b_send[ex, t, pl.ds(mine, 16)]

    def wait_b(ex, t):
        part = b_recv.at[ex, t, pl.ds(0, 496)]
        copy(part, part, b_sem.at[ex, t], (rd, c)).wait_recv()

    def rows_0(e):
        copy(zr.at[e], zr.at[e], in_sem.at[e], (rd, c)).wait_recv()
        grid[...] = attend(zr[e], 0, 0)
        send_a(0, e, True)

    loop(0, 2, rows_0)
    send_b(0)

    def columns_0(t):
        wait_b(0, t)
        grid[...] = attend(b_recv[0, t], 0, 1)
        zc[t] = grid[...].astype(BF)
        send_a(1, t, False)

    loop(0, 2, columns_0)
    send_b(1)

    def rows_1(e):
        wait_b(1, e)
        symmetric = (0.5 * (zc[e].astype(F32) + b_recv[1, e].astype(F32))).astype(BF)
        grid[...] = attend(transition(symmetric.astype(F32), 0), 1, 0)
        send_a(2, e, False)

    loop(0, 2, rows_1)
    send_b(2)

    spot = pl.multiple_of((cy * 8 + zh * 4 + cx) * 16, 16)

    def columns_1(t):
        wait_b(2, t)
        grid[...] = attend(b_recv[2, t], 1, 1)
        for s in range(8):
            for e in range(2):
                part = grid[pl.ds((s // 2) * 128 + (s % 2) * 2 + e, 32, stride=4), :]
                a_send[3, s, t, e * 32 : e * 32 + 32, :] = part.astype(BF)
                mix[pl.ds(s * 2 + e, 32, stride=16), :] = part

        def go_t(k):
            s = (r + k) % 8
            copy(a_send.at[3, s, t], a_recv.at[3, rd, t], t_sem.at[t], (s, c)).start()

        loop(1, 8, go_t)
        a_recv[3, rd, t] = a_send[3, r, t]
        b_send[3, t] = mix[0:512, :].astype(BF)

        def go_m(k):
            w = (c + k) % 32
            rows = pl.ds(pl.multiple_of(((w // 8) * 8 + (w % 2) * 4 + (w // 2) % 4) * 16, 16), 16)
            copy(b_send.at[3, t, rows], b_recv.at[3, t, pl.ds(spot, 16)], m_sem.at[t], (rd, w)).start()

        loop(0, 32, go_m)

    loop(0, 2, columns_1)

    for t in range(2):
        part = a_recv.at[3, pl.ds(0, 7), t]
        copy(part, part, t_sem.at[t], (rd, c)).wait_recv()
    for e in range(2):
        for s in range(8):
            for t in range(2):
                mix[pl.ds(e * 512 + s * 2 + t, 32, stride=16), :] = a_recv[
                    3, s, t, e * 32 : e * 32 + 32, :
                ].astype(F32)
        copy(b_recv.at[3, e], b_recv.at[3, e], m_sem.at[e], (rd, c)).wait_recv()
        symmetric = (0.5 * (mix[e * 512 : e * 512 + 512, :] + b_recv[3, e].astype(F32))).astype(BF)
        final = transition(symmetric.astype(F32), 1)
        for y in range(4):
            for h in range(2):
                for q in range(4):
                    block = (y * 8 + h * 4 + q) * 16
                    out[y * 8 + q * 2 + h, e] = final[block : block + 16]

    for e in range(2):
        copy(zr.at[e], zr.at[e], in_sem.at[e], (rd, c)).wait_send()
        copy(b_recv.at[3, e], b_recv.at[3, e], m_sem.at[e], (rd, c)).wait_send()
        for ex in range(4):
            part = a_send.at[ex, pl.ds(0, 7), e]
            copy(part, part, t_sem.at[e], (rd, c)).wait_send()
        for ex in range(3):
            part = b_send.at[ex, e, pl.ds(0, 496)]
            copy(part, part, t_sem.at[e], (rd, c)).wait_send()


def local(pair, *weights):
    vmem = pltpu.VMEM
    dma = pltpu.SemaphoreType.DMA
    tile = pair.reshape(32, 2, 16, CHANNELS)
    result = pl.pallas_call(
        kernel,
        out_shape=jax.ShapeDtypeStruct(tile.shape, BF),
        in_specs=[pl.BlockSpec(memory_space=vmem)] * 8,
        out_specs=pl.BlockSpec(memory_space=vmem),
        scratch_shapes=[
            vmem((2, 2, INNER, CHANNELS), BF),
            vmem((2, 2, INNER, CHANNELS), BF),
            vmem((2, 2, INNER, CHANNELS), BF),
            vmem((INNER, LENGTH), BF),
            vmem((LENGTH, INNER), BF),
            vmem((HEADS, 48, LENGTH), BF),
            vmem((INNER, LENGTH), F32),
            vmem((INNER, LENGTH), BF),
            vmem((LENGTH, CHANNELS), F32),
            vmem((2 * LENGTH, CHANNELS), F32),
            vmem((2, LENGTH, CHANNELS), BF),
            vmem((2, LENGTH, CHANNELS), BF),
            vmem((4, 8, 2, 64, CHANNELS), BF),
            vmem((4, 8, 2, 64, CHANNELS), BF),
            vmem((4, 2, LENGTH, CHANNELS), BF),
            vmem((4, 2, LENGTH, CHANNELS), BF),
            dma,
            dma((2,)),
            dma((3, 2)),
            dma((3, 2)),
            dma((2,)),
            dma((2,)),
        ],
        compiler_params=pltpu.CompilerParams(
            collective_id=0, has_side_effects=True, vmem_limit_bytes=48 << 20
        ),
    )(tile, *weights)
    return result.reshape(pair.shape)


def solution(mesh):
    return jax.shard_map(
        local,
        mesh=mesh,
        in_specs=(P(None, "row", None, "col", None), P(), P(), P(), P(), P(), P(), P()),
        out_specs=P(None, "row", None, "col", None),
        check_vma=False,
    )
```

time: 311 us -> 102 us (0.33)
  Pallas kernels: 0 us -> 92.6 us
  blocking collectives: 79.3 us -> 0 us
  matrix products: 66.6 us -> 0 us
  waiting for transfers between devices: 59.2 us -> 0 us
  starting transfers between devices: 45.5 us -> 0 us
  other arithmetic: 40.8 us -> 0 us
  local copies, waits for them, and re-layouts: 16 us -> 8.3 us
    pallas_call x0 -> x1, Pallas kernels: none -> 92.6 us  [local(): pl.pallas_call(kernel, out_shape=jax.ShapeDtypeStruct(tile.shape, BF), in...]
    all_to_all x6 -> x0, blocking collectives: 79.3 us -> none  [the longest x2 30.8 us: layer_step(): lax.all_to_all(row_slab.reshape(1, span_rows, length, channels), 'col', s...]
    dot_general x22 -> x0, matrix products: 66.6 us -> none  [the longest x4 29.3 us: attend(): jnp.einsum('ehqd,ehkd->ehqk', queries, key_rows, preferred_element_type=j...]
    all_to_all x6 -> x0, waiting for transfers between devices: 59.2 us -> none  [the longest x2 24.6 us: layer_step(): lax.all_to_all(column_view.reshape(col_count, col_width, span_rows, chann...]
    all_to_all x6 -> x0, starting transfers between devices: 45.5 us -> none  [the longest x2 19.4 us: layer_step(): lax.all_to_all(pair_tile, 'row', split_axis=2, concat_axis=1, tiled=True)]
    reduce_sum x16 -> x0, other arithmetic: 38.4 us -> none  [the longest x4 34.2 us: attend(): denominator = jnp.sum(exponent, axis=-1, keepdims=True)]
    unnamed x1 -> x17, local copies, waits for them, and re-layouts: 1.67 us -> 8.3 us
    slice x6 -> x0, local copies, waits for them, and re-layouts: 5.63 us -> none  [the longest x2 1.92 us: attend(): weights[0][direction]]
  transfers between devices with their start and end apart: 6 -> 0, of which waited for: 6 -> 0; matrix products, arithmetic and copies ran while one was open for 3% -> 0% of each run, Pallas kernels for 0% -> 0%
where the time goes in v1:
time: 102 us; the launch traced here: 101 us
  Pallas kernels  92.6 us (91%)
  local copies, waits for them, and re-layouts  8.3 us (8%)
    pallas_call x1, Pallas kernels, local(): pl.pallas_call(kernel, out_shape=jax.ShapeDtypeStruct(tile.shape, BF), in...  92.6 us
    unnamed x17, local copies, waits for them, and re-layouts  8.3 us

profile of v1, /device:TPU:1, one launch (start us, length us, event | category | flops | bytes accessed | tf_op | source)
XLA Modules:
  0.0 100.9 jit_solution(4379632867598886244)
XLA Ops:
  0.0 0.0 copy-start
  0.0 0.9 copy-done
  1.0 0.0 copy-start.1
  1.0 0.9 copy-done.1
  1.9 0.0 copy-start.2
  1.9 0.9 copy-done.2
  2.9 0.0 copy-start.3
  2.9 0.9 copy-done.3
  3.8 0.0 copy-start.4
  3.8 0.9 copy-done.4
  4.8 0.0 copy-start.5
  4.8 0.9 copy-done.5
  5.7 0.0 copy-start.6
  5.7 0.9 copy-done.6
  6.7 0.0 copy-start.7
  6.7 0.9 copy-done.7
  7.6 92.6 %shard_map.82 = bf16[32,2,16,128]{3,2,1,0:T(8,128)(2,1)S(1)} custom-call(bf16[32,2,16,128]{3,2,1,0:T(8,128)(2,1)S(1)} %bitcast.5, bf16[2,2,128,256]{3,2,1,0:T(8,128)(2,1)S(1)} %copy-done.1, bf16[2,2,128,256]{3,2,1,0:T(8,128)(2,1)S(1)} %copy-done.2, bf16[2,2,128,256]{3,2,1,0:T(8,128)(2,1)S(1)} %copy-done.3, bf16[2,2,128,256]{3,2,1,0:T(8,128)(2,1)S(1)} %copy-done.4, ...), custom_call_target="tpu_custom_call" | custom-call | tf_op jit(solution)/shard_map/pallas_call | solution.py:251
  100.2 0.7 copy.11
Async XLA Ops:
  0.0 0.9 copy-start
  1.0 0.9 copy-start.1
  1.9 0.9 copy-start.2
  2.9 0.9 copy-start.3
  3.8 0.9 copy-start.4
  4.8 0.9 copy-start.5
  5.7 0.9 copy-start.6
  6.7 0.9 copy-start.7

commit v2 on v1

v2 whole, which is shorter than its diff:
```python
import math

import jax
import jax.numpy as jnp
from jax import lax
from jax.experimental import pallas as pl
from jax.experimental.pallas import tpu as pltpu
from jax.sharding import PartitionSpec as P

HEADS = 8
HEAD_DIM = 32
INNER = HEADS * HEAD_DIM
CHANNELS = 128
LENGTH = 512
EPSILON = 1e-05
SCALE = math.log2(math.e) / math.sqrt(HEAD_DIM)
MESH = pl.DeviceIdType.MESH
BF = jnp.bfloat16
F32 = jnp.float32
NT = (((1,), (1,)), ((), ()))
TN = (((0,), (0,)), ((), ()))


def layer_norm(wide):
    center = wide - jnp.mean(wide, axis=-1, keepdims=True)
    spread = jnp.mean(center * center, axis=-1, keepdims=True)
    return (center * lax.rsqrt(spread + EPSILON)).astype(BF)


def kernel(
    x, hbm_query, hbm_key, hbm_value, hbm_gate, hbm_out, hbm_in, hbm_back, out,
    w_query, w_key, w_value, w_gate, w_out, w_in, w_back,
    wqt, wvt, wgt, qt, kr, vt, gt, go, grid, mix, stage,
    token, zcol, a_send, a_recv, b_send, inbox, t_send, t_recv, m_send, m_recv,
    send_sem, in_sem, a_sem, b_sem, t_sem, m_sem, w_sem,
):
    r = lax.axis_index("row")
    c = lax.axis_index("col")
    core = r % 2
    cy = c // 8
    cx = (c // 2) % 4
    zh = c % 2
    rd = (r + 4) % 8
    ga = cx * 2 + core
    gb = (rd // 2) * 8 + cy * 2 + zh

    def peer_a(g):
        return (r - core + g % 2, cy * 8 + (g // 2) * 2 + zh)

    def peer_b(g):
        return (((g // 8 + 2) % 4) * 2 + core, ((g // 2) % 4) * 8 + cx * 2 + g % 2)

    def copy(src, dst, sem, device):
        return pltpu.make_async_remote_copy(src, dst, send_sem, sem, device_id=device, device_id_type=MESH)

    def loop(start, stop, body):
        lax.fori_loop(start, stop, lambda k, carry: (body(k), carry)[1], 0)

    barrier = pltpu.get_barrier_semaphore()
    loop(0, 32, lambda k: pl.semaphore_signal(barrier, inc=1, device_id=(rd, k), device_id_type=MESH))
    loop(1, 8, lambda k: pl.semaphore_signal(barrier, inc=1, device_id=((r + k) % 8, c), device_id_type=MESH))
    fetches = [
        pltpu.make_async_copy(source, target, w_sem.at[i])
        for i, (source, target) in enumerate(
            (
                (hbm_query, w_query),
                (hbm_value, w_value),
                (hbm_gate, w_gate),
                (hbm_key, w_key),
                (hbm_out, w_out),
                (hbm_in, w_in),
                (hbm_back, w_back),
            )
        )
    ]
    for fetch in fetches:
        fetch.start()
    pl.semaphore_wait(barrier, 39)

    place = pl.multiple_of((cx * 8 + cy * 2 + zh) * 16, 16)
    for e in range(2):

        def send_rows(k):
            d = (c + k) % 32
            copy(x.at[d, e], inbox.at[0, e, pl.ds(place, 16)], in_sem.at[0, e], (rd, d)).start()

        loop(0, 32, send_rows)

    for fetch in fetches:
        fetch.wait()
    for l in range(2):
        for n in range(2):
            for source, target in ((w_query, wqt), (w_value, wvt), (w_gate, wgt)):
                target[l, n] = source[l, n].astype(F32).T.astype(BF)
    vt[...] = jnp.ones_like(vt)

    def project(l, n):
        normed = layer_norm(token[...])
        qt[...] = (lax.dot_general(wqt[l, n], normed, NT, preferred_element_type=F32) * SCALE).astype(BF)
        kr[...] = jnp.dot(normed, w_key[l, n], preferred_element_type=F32).astype(BF)
        value_rows = lax.dot_general(wvt[l, n], normed, NT, preferred_element_type=F32).astype(BF)
        for h in range(HEADS):
            vt[h, 0:HEAD_DIM, :] = value_rows[h * HEAD_DIM : (h + 1) * HEAD_DIM]
        gt[...] = jax.nn.sigmoid(lax.dot_general(wgt[l, n], normed, NT, preferred_element_type=F32))

    def attend(l, n, first, count):
        span = slice(first, first + count)

        def scores_of(h):
            rows = slice(h * HEAD_DIM, (h + 1) * HEAD_DIM)
            return jnp.dot(kr[:, rows], qt[rows, span], preferred_element_type=F32)

        def probs_of(scores):
            return jnp.exp2(scores - jnp.max(scores, axis=0, keepdims=True)).astype(BF)

        def blend(h, probs):
            rows = slice(h * HEAD_DIM, (h + 1) * HEAD_DIM)
            total = jnp.dot(vt[h], probs, preferred_element_type=F32)
            go[rows, span] = (gt[rows, span] * total[:HEAD_DIM] / total[HEAD_DIM : HEAD_DIM + 1]).astype(BF)

        scores = scores_of(0)
        probs = None
        for h in range(HEADS):
            later = scores_of(h + 1) if h + 1 < HEADS else None
            fresh = probs_of(scores)
            if probs is not None:
                blend(h - 1, probs)
            probs, scores = fresh, later
        blend(HEADS - 1, probs)
        update = lax.dot_general(go[:, span], w_out[l, n], TN, preferred_element_type=F32)
        grid[span, :] = token[span, :] + update

    def transition(wide, l):
        normed = layer_norm(wide)
        hidden = jax.nn.relu(jnp.dot(normed, w_in[l], preferred_element_type=F32)).astype(BF)
        return (wide + jnp.dot(hidden, w_back[l], preferred_element_type=F32)).astype(BF)

    def send_a(p, e, t):
        @pl.when(p == 0)
        def first_order():
            for g in range(8):
                for q in range(4):
                    start = t * 256 + (g // 2) * 64 + q * 2 + g % 2
                    stage[g * 32 + q * 8 : g * 32 + q * 8 + 8, :] = grid[pl.ds(start, 8, stride=8), :]

        @pl.when(p > 0)
        def later_order():
            for g in range(8):
                stage[g * 32 : g * 32 + 32, :] = grid[pl.ds(t * 256 + g, 32, stride=8), :]

        for g in range(8):
            a_send[p, e, t, g] = stage[g * 32 : g * 32 + 32, :].astype(BF)

        def go_a(k):
            g = (ga + k) % 8
            copy(a_send.at[p, e, t, g], a_recv.at[p, e, t, ga], a_sem.at[p, e, t], peer_a(g)).start()

        loop(1, 8, go_a)
        a_recv[p, e, t, ga] = a_send[p, e, t, ga]

    mine = pl.ds(pl.multiple_of(gb * 16, 16), 16)

    def send_b(p):
        for t in range(2):
            for e in range(2):
                part = a_recv.at[p, e, t, pl.ds(0, 7)]
                copy(part, part, a_sem.at[p, e, t], (rd, c)).wait_recv()
                for g in range(8):
                    mix[pl.ds(e * 8 + g, 32, stride=16), :] = a_recv[p, e, t, g].astype(F32)
            b_send[p, t] = mix[...].astype(BF)

            def go_b(k):
                g = (gb + k) % 32
                rows = pl.ds(pl.multiple_of(g * 16, 16), 16)
                copy(b_send.at[p, t, rows], inbox.at[p + 1, t, mine], b_sem.at[p, t], peer_b(g)).start()

            loop(1, 32, go_b)
            inbox[p + 1, t, mine] = b_send[p, t, mine]

    spot = pl.ds(place, 16)

    def send_tiles(t, e):
        for s in range(8):
            for q in range(4):
                start = e * 256 + (s // 2) * 64 + q * 2 + s % 2
                stage[s * 32 + q * 8 : s * 32 + q * 8 + 8, :] = grid[pl.ds(start, 8, stride=8), :]
        for s in range(8):
            t_send[e, t, s] = stage[s * 32 : s * 32 + 32, :].astype(BF)

        def go_t(k):
            s = (r + k) % 8
            copy(t_send.at[e, t, s], t_recv.at[e, t, rd], t_sem.at[e, t], (s, c)).start()

        loop(1, 8, go_t)
        t_recv[e, t, rd] = t_send[e, t, r]
        for s in range(8):
            mix[pl.ds(s * 2 + e, 32, stride=16), :] = stage[s * 32 : s * 32 + 32, :]

    def send_mirrored(t):
        m_send[t] = mix[...].astype(BF)

        def go_m(k):
            w = (c + k) % 32
            rows = pl.ds(pl.multiple_of((((w // 2) % 4) * 8 + (w // 8) * 2 + w % 2) * 16, 16), 16)
            copy(m_send.at[t, rows], m_recv.at[t, spot], m_sem.at[t], (rd, w)).start()

        loop(0, 32, go_m)

    def step(k):
        p = k // 2
        e = k % 2

        @pl.when(p == 0)
        def first_input():
            copy(inbox.at[0, e], inbox.at[0, e], in_sem.at[0, e], (rd, c)).wait_recv()
            mix[...] = inbox[0, e].astype(F32)
            for t in range(2):
                token[t * 256 : t * 256 + 256, :] = mix[pl.ds(t, 256, stride=2), :]

        @pl.when(p > 0)
        def later_input():
            part = inbox.at[p, e, pl.ds(0, 496)]
            copy(part, part, b_sem.at[p - 1, e], (rd, c)).wait_recv()
            for g in range(32):
                block = inbox[p, e, g * 16 : g * 16 + 16, :].astype(F32)
                for t in range(2):
                    token[t * 256 + g * 8 : t * 256 + g * 8 + 8, :] = block[t * 8 : t * 8 + 8]

        @pl.when(p == 2)
        def symmetrize():
            symmetric = (0.5 * (zcol[e].astype(F32) + token[...])).astype(BF)
            token[...] = transition(symmetric.astype(F32), 0).astype(F32)

        l = p // 2
        n = p % 2
        project(l, n)

        def send(t):
            @pl.when(p < 3)
            def exchange():
                send_a(p, e, t)

            @pl.when(p == 3)
            def finish():
                send_tiles(e, t)

        @pl.when(e == 0)
        def whole():
            attend(l, n, 0, 512)
            send(0)
            send(1)

        @pl.when(e == 1)
        def halves():
            attend(l, n, 0, 256)
            send(0)
            attend(l, n, 256, 256)
            send(1)

        @pl.when((p < 3) & (e == 1))
        def forward():
            send_b(p)

        @pl.when(p == 3)
        def mirror():
            send_mirrored(e)

        @pl.when(p == 1)
        def keep():
            zcol[e] = grid[...].astype(BF)

    loop(0, 8, step)

    def tile(e):
        for t in range(2):
            part = t_recv.at[e, t, pl.ds(0, 7)]
            copy(part, part, t_sem.at[e, t], (rd, c)).wait_recv()
            for s in range(8):
                mix[pl.ds(s * 2 + t, 32, stride=16), :] = t_recv[e, t, s].astype(F32)
        copy(m_recv.at[e], m_recv.at[e], m_sem.at[e], (rd, c)).wait_recv()
        symmetric = (0.5 * (mix[...] + m_recv[e].astype(F32))).astype(BF)
        final = transition(symmetric.astype(F32), 1)
        for q in range(4):
            for y in range(4):
                for h in range(2):
                    block = (q * 8 + y * 2 + h) * 16
                    out[y * 8 + q * 2 + h, e] = final[block : block + 16]

    loop(0, 2, tile)

    for e in range(2):
        copy(inbox.at[0, e], inbox.at[0, e], in_sem.at[0, e], (rd, c)).wait_send()
        copy(m_send.at[e], m_send.at[e], m_sem.at[e], (rd, c)).wait_send()
        for t in range(2):
            part = t_send.at[e, t, pl.ds(0, 7)]
            copy(part, part, in_sem.at[0, e], (rd, c)).wait_send()
        for p in range(3):
            for t in range(2):
                part = a_send.at[p, e, t, pl.ds(0, 7)]
                copy(part, part, in_sem.at[0, e], (rd, c)).wait_send()
            part = b_send.at[p, e, pl.ds(0, 496)]
            copy(part, part, in_sem.at[0, e], (rd, c)).wait_send()


def local(pair, *weights):
    vmem = pltpu.VMEM
    dma = pltpu.SemaphoreType.DMA
    tile = pair.reshape(32, 2, 16, CHANNELS)
    result = pl.pallas_call(
        kernel,
        out_shape=jax.ShapeDtypeStruct(tile.shape, BF),
        in_specs=[pl.BlockSpec(memory_space=pltpu.HBM)] * 8,
        out_specs=pl.BlockSpec(memory_space=vmem),
        scratch_shapes=[vmem(weight.shape, BF) for weight in weights]
        + [
            vmem((2, 2, INNER, CHANNELS), BF),
            vmem((2, 2, INNER, CHANNELS), BF),
            vmem((2, 2, INNER, CHANNELS), BF),
            vmem((INNER, LENGTH), BF),
            vmem((LENGTH, INNER), BF),
            vmem((HEADS, 48, LENGTH), BF),
            vmem((INNER, LENGTH), F32),
            vmem((INNER, LENGTH), BF),
            vmem((LENGTH, CHANNELS), F32),
            vmem((LENGTH, CHANNELS), F32),
            vmem((LENGTH, CHANNELS), F32),
            vmem((LENGTH, CHANNELS), F32),
            vmem((2, LENGTH, CHANNELS), BF),
            vmem((3, 2, 2, 8, 32, CHANNELS), BF),
            vmem((3, 2, 2, 8, 32, CHANNELS), BF),
            vmem((3, 2, LENGTH, CHANNELS), BF),
            vmem((4, 2, LENGTH, CHANNELS), BF),
            vmem((2, 2, 8, 32, CHANNELS), BF),
            vmem((2, 2, 8, 32, CHANNELS), BF),
            vmem((2, LENGTH, CHANNELS), BF),
            vmem((2, LENGTH, CHANNELS), BF),
            dma,
            dma((1, 2)),
            dma((3, 2, 2)),
            dma((3, 2)),
            dma((2, 2)),
            dma((2,)),
            dma((7,)),
        ],
        compiler_params=pltpu.CompilerParams(
            collective_id=0, has_side_effects=True, vmem_limit_bytes=62 << 20
        ),
    )(tile, *weights)
    return result.reshape(pair.shape)


def solution(mesh):
    return jax.shard_map(
        local,
        mesh=mesh,
        in_specs=(P(None, "row", None, "col", None), P(), P(), P(), P(), P(), P(), P()),
        out_specs=P(None, "row", None, "col", None),
        check_vma=False,
    )
```

time: 102 us -> 95.9 us (0.940)
  local copies, waits for them, and re-layouts: 8.3 us -> 1.67 us
  Pallas kernels: 92.6 us -> 94.1 us
    unnamed x17 -> x1, local copies, waits for them, and re-layouts: 8.3 us -> 1.67 us
    pallas_call x1, Pallas kernels: 92.6 us -> 94.1 us  [local(): pl.pallas_call(kernel, out_shape=jax.ShapeDtypeStruct(tile.shape, BF), in...]
where the time goes in v2:
time: 95.9 us; the launch traced here: 95.8 us
  Pallas kernels  94.1 us (98%)
  local copies, waits for them, and re-layouts  1.67 us (2%)
    pallas_call x1, Pallas kernels, local(): pl.pallas_call(kernel, out_shape=jax.ShapeDtypeStruct(tile.shape, BF), in...  94.1 us

profile of v2, /device:TPU:1, one launch (start us, length us, event | category | flops | bytes accessed | tf_op | source)
XLA Modules:
  0.0 95.8 jit_solution(11617350870487857265)
XLA Ops:
  0.0 94.1 %shard_map.82 = bf16[32,2,16,128]{3,2,1,0:T(8,128)(2,1)} custom-call(bf16[32,2,16,128]{3,2,1,0:T(8,128)(2,1)} %bitcast.5, bf16[2,2,128,256]{3,2,1,0:T(8,128)(2,1)} %hbm_query.1, bf16[2,2,128,256]{3,2,1,0:T(8,128)(2,1)} %hbm_key.1, bf16[2,2,128,256]{3,2,1,0:T(8,128)(2,1)} %hbm_value.1, bf16[2,2,128,256]{3,2,1,0:T(8,128)(2,1)} %hbm_gate.1, ...), custom_call_target="tpu_custom_call" | custom-call | tf_op jit(solution)/shard_map/pallas_call | solution.py:309
  94.1 1.7 %copy.11 = bf16[32,1,2,16,128]{4,3,2,1,0:T(8,128)(2,1)} copy(bf16[32,1,2,16,128]{4,3,2,1,0:T(8,128)(2,1)} %bitcast.4) | data formatting | bytes 524288

commit v3 on v2

--- a/solution.py
+++ b/solution.py
@@ -116,7 +116,8 @@
         def blend(h, probs):
             rows = slice(h * HEAD_DIM, (h + 1) * HEAD_DIM)
             total = jnp.dot(vt[h], probs, preferred_element_type=F32)
-            go[rows, span] = (gt[rows, span] * total[:HEAD_DIM] / total[HEAD_DIM : HEAD_DIM + 1]).astype(BF)
+            inverse = 1.0 / total[HEAD_DIM : HEAD_DIM + 1]
+            go[rows, span] = (gt[rows, span] * (total[:HEAD_DIM] * inverse)).astype(BF)
 
         scores = scores_of(0)
         probs = None
@@ -160,22 +161,22 @@
 
     mine = pl.ds(pl.multiple_of(gb * 16, 16), 16)
 
-    def send_b(p):
-        for t in range(2):
-            for e in range(2):
-                part = a_recv.at[p, e, t, pl.ds(0, 7)]
-                copy(part, part, a_sem.at[p, e, t], (rd, c)).wait_recv()
-                for g in range(8):
-                    mix[pl.ds(e * 8 + g, 32, stride=16), :] = a_recv[p, e, t, g].astype(F32)
-            b_send[p, t] = mix[...].astype(BF)
-
-            def go_b(k):
-                g = (gb + k) % 32
-                rows = pl.ds(pl.multiple_of(g * 16, 16), 16)
-                copy(b_send.at[p, t, rows], inbox.at[p + 1, t, mine], b_sem.at[p, t], peer_b(g)).start()
-
-            loop(1, 32, go_b)
-            inbox[p + 1, t, mine] = b_send[p, t, mine]
+    def build_b(p, t):
+        for e in range(2):
+            part = a_recv.at[p, e, t, pl.ds(0, 7)]
+            copy(part, part, a_sem.at[p, e, t], (rd, c)).wait_recv()
+            for g in range(8):
+                mix[pl.ds(e * 8 + g, 32, stride=16), :] = a_recv[p, e, t, g].astype(F32)
+        b_send[p, t] = mix[...].astype(BF)
+        inbox[p + 1, t, mine] = b_send[p, t, mine]
+
+    def start_b(p, t):
+        def go_b(k):
+            g = (gb + k) % 32
+            rows = pl.ds(pl.multiple_of(g * 16, 16), 16)
+            copy(b_send.at[p, t, rows], inbox.at[p + 1, t, mine], b_sem.at[p, t], peer_b(g)).start()
+
+        loop(1, 32, go_b)
 
     spot = pl.ds(place, 16)
 
@@ -221,6 +222,11 @@
         def later_input():
             part = inbox.at[p, e, pl.ds(0, 496)]
             copy(part, part, b_sem.at[p - 1, e], (rd, c)).wait_recv()
+
+            @pl.when(e == 0)
+            def second():
+                start_b(p - 1, 1)
+
             for g in range(32):
                 block = inbox[p, e, g * 16 : g * 16 + 16, :].astype(F32)
                 for t in range(2):
@@ -259,7 +265,9 @@
 
         @pl.when((p < 3) & (e == 1))
         def forward():
-            send_b(p)
+            build_b(p, 0)
+            start_b(p, 0)
+            build_b(p, 1)
 
         @pl.when(p == 3)
         def mirror():

time: 95.9 us -> 101 us (1.053)
  Pallas kernels: 94.1 us -> 98.9 us
    pallas_call x1, Pallas kernels: 94.1 us -> 98.9 us  [local(): pl.pallas_call(kernel, out_shape=jax.ShapeDtypeStruct(tile.shape, BF), in...]
where the time goes in v3:
time: 101 us
  Pallas kernels  98.9 us (98%)
  local copies, waits for them, and re-layouts  1.67 us (2%)
    pallas_call x1, Pallas kernels, local(): pl.pallas_call(kernel, out_shape=jax.ShapeDtypeStruct(tile.shape, BF), in...  98.9 us

profile of v3, /device:TPU:1, one launch (start us, length us, event | category | flops | bytes accessed | tf_op | source)
XLA Modules:
  0.0 100.6 jit_solution(17822812636883979756)
XLA Ops:
  0.0 98.9 %shard_map.82 = bf16[32,2,16,128]{3,2,1,0:T(8,128)(2,1)} custom-call(bf16[32,2,16,128]{3,2,1,0:T(8,128)(2,1)} %bitcast.5, bf16[2,2,128,256]{3,2,1,0:T(8,128)(2,1)} %hbm_query.1, bf16[2,2,128,256]{3,2,1,0:T(8,128)(2,1)} %hbm_key.1, bf16[2,2,128,256]{3,2,1,0:T(8,128)(2,1)} %hbm_value.1, bf16[2,2,128,256]{3,2,1,0:T(8,128)(2,1)} %hbm_gate.1, ...), custom_call_target="tpu_custom_call" | custom-call | tf_op jit(solution)/shard_map/pallas_call | solution.py:317
  98.9 1.7 %copy.11 = bf16[32,1,2,16,128]{4,3,2,1,0:T(8,128)(2,1)} copy(bf16[32,1,2,16,128]{4,3,2,1,0:T(8,128)(2,1)} %bitcast.4) | data formatting | bytes 524288

commit v4 on v2

--- a/solution.py
+++ b/solution.py
@@ -116,7 +116,8 @@
         def blend(h, probs):
             rows = slice(h * HEAD_DIM, (h + 1) * HEAD_DIM)
             total = jnp.dot(vt[h], probs, preferred_element_type=F32)
-            go[rows, span] = (gt[rows, span] * total[:HEAD_DIM] / total[HEAD_DIM : HEAD_DIM + 1]).astype(BF)
+            inverse = 1.0 / total[HEAD_DIM : HEAD_DIM + 1]
+            go[rows, span] = (gt[rows, span] * (total[:HEAD_DIM] * inverse)).astype(BF)
 
         scores = scores_of(0)
         probs = None

time: 95.9 us -> 96.1 us (level)
  no operation moved by 1% of the time
where the time goes in v4:
time: 96.1 us; the launch traced here: 96 us
  Pallas kernels  94.3 us (98%)
  local copies, waits for them, and re-layouts  1.67 us (2%)
    pallas_call x1, Pallas kernels, local(): pl.pallas_call(kernel, out_shape=jax.ShapeDtypeStruct(tile.shape, BF), in...  94.3 us

profile of v4, /device:TPU:1, one launch (start us, length us, event | category | flops | bytes accessed | tf_op | source)
XLA Modules:
  0.0 96.0 jit_solution(18259673667522957751)
XLA Ops:
  0.0 94.3 %shard_map.82 = bf16[32,2,16,128]{3,2,1,0:T(8,128)(2,1)} custom-call(bf16[32,2,16,128]{3,2,1,0:T(8,128)(2,1)} %bitcast.5, bf16[2,2,128,256]{3,2,1,0:T(8,128)(2,1)} %hbm_query.1, bf16[2,2,128,256]{3,2,1,0:T(8,128)(2,1)} %hbm_key.1, bf16[2,2,128,256]{3,2,1,0:T(8,128)(2,1)} %hbm_value.1, bf16[2,2,128,256]{3,2,1,0:T(8,128)(2,1)} %hbm_gate.1, ...), custom_call_target="tpu_custom_call" | custom-call | tf_op jit(solution)/shard_map/pallas_call | solution.py:310
  94.3 1.7 %copy.11 = bf16[32,1,2,16,128]{4,3,2,1,0:T(8,128)(2,1)} copy(bf16[32,1,2,16,128]{4,3,2,1,0:T(8,128)(2,1)} %bitcast.4) | data formatting | bytes 524288

commit v5 on v2

--- a/solution.py
+++ b/solution.py
@@ -81,7 +81,7 @@
     for e in range(2):
 
         def send_rows(k):
-            d = (c + k) % 32
+            d = (c + k * 13) % 32
             copy(x.at[d, e], inbox.at[0, e, pl.ds(place, 16)], in_sem.at[0, e], (rd, d)).start()
 
         loop(0, 32, send_rows)
@@ -170,7 +170,7 @@
             b_send[p, t] = mix[...].astype(BF)
 
             def go_b(k):
-                g = (gb + k) % 32
+                g = (gb + k * 13) % 32
                 rows = pl.ds(pl.multiple_of(g * 16, 16), 16)
                 copy(b_send.at[p, t, rows], inbox.at[p + 1, t, mine], b_sem.at[p, t], peer_b(g)).start()
 
@@ -200,7 +200,7 @@
         m_send[t] = mix[...].astype(BF)
 
         def go_m(k):
-            w = (c + k) % 32
+            w = (c + k * 13) % 32
             rows = pl.ds(pl.multiple_of((((w // 2) % 4) * 8 + (w // 8) * 2 + w % 2) * 16, 16), 16)
             copy(m_send.at[t, rows], m_recv.at[t, spot], m_sem.at[t], (rd, w)).start()
 

time: 95.9 us -> 97.7 us (1.019)
  Pallas kernels: 94.1 us -> 95.9 us
    pallas_call x1, Pallas kernels: 94.1 us -> 95.9 us  [local(): pl.pallas_call(kernel, out_shape=jax.ShapeDtypeStruct(tile.shape, BF), in...]
where the time goes in v5:
time: 97.7 us; the launch traced here: 97.6 us
  Pallas kernels  95.9 us (98%)
  local copies, waits for them, and re-layouts  1.67 us (2%)
    pallas_call x1, Pallas kernels, local(): pl.pallas_call(kernel, out_shape=jax.ShapeDtypeStruct(tile.shape, BF), in...  95.9 us

profile of v5, /device:TPU:1, one launch (start us, length us, event | category | flops | bytes accessed | tf_op | source)
XLA Modules:
  0.0 97.6 jit_solution(15874880325177468975)
XLA Ops:
  0.0 95.9 %shard_map.82 = bf16[32,2,16,128]{3,2,1,0:T(8,128)(2,1)} custom-call(bf16[32,2,16,128]{3,2,1,0:T(8,128)(2,1)} %bitcast.5, bf16[2,2,128,256]{3,2,1,0:T(8,128)(2,1)} %hbm_query.1, bf16[2,2,128,256]{3,2,1,0:T(8,128)(2,1)} %hbm_key.1, bf16[2,2,128,256]{3,2,1,0:T(8,128)(2,1)} %hbm_value.1, bf16[2,2,128,256]{3,2,1,0:T(8,128)(2,1)} %hbm_gate.1, ...), custom_call_target="tpu_custom_call" | custom-call | tf_op jit(solution)/shard_map/pallas_call | solution.py:309
  95.9 1.7 %copy.11 = bf16[32,1,2,16,128]{4,3,2,1,0:T(8,128)(2,1)} copy(bf16[32,1,2,16,128]{4,3,2,1,0:T(8,128)(2,1)} %bitcast.4) | data formatting | bytes 524288
